TPU v7x, 128 devices: a whole 4x4x4 slice. The times are simulated.
128 devices in a mesh: dp: 16 (over y, x_lo, core), mp: 8 (over x_hi, z).
Axes of the slice: x: 4 (x_hi: 2, x_lo: 2; x = x_hi * 2 + x_lo), y: 4, z: 4, core: 2. Of those that a mesh axis runs over, the one named last changes fastest.
Arguments:
- grads: bfloat16 [16, 4096, 8192], P('dp', None, 'mp'), may hold values from -6 to 6
- projector: bfloat16 [8192, 1024], P('mp'), may hold values from -0.0625 to 0.0625
- moment: float32 [4096, 1024], P(('dp', 'mp')), may hold values from -1.2 to 1.2
- second: float32 [4096, 1024], P(('dp', 'mp')), may hold values from 0.0001 to 0.01
Outputs:
- new_moment: float32 [4096, 1024], P(('dp', 'mp'))
- new_second: float32 [4096, 1024], P(('dp', 'mp'))
- update: bfloat16 [4096, 8192], P(None, 'mp')
All inputs are finite; a program needn't handle non-finite values.
Results may differ from a plain program's by a relative error of at most 0.01.
Values may be sent and summed in bfloat16 or wider, within the bound.
A program may use at most 128 MiB of HBM per device.

v0:
```python
import jax
import jax.numpy as jnp
from jax import lax
from jax.sharding import PartitionSpec as P

ADAM_STEP = 10


def decode_rows(dir_rows, projector):
    return lax.dot_general(
        dir_rows, projector, (((1,), (1,)), ((), ())), preferred_element_type=jnp.float32
    ).astype(jnp.bfloat16)


def shards(grads, projector, moment, second):
    grad_local = grads[0]
    replicas = lax.axis_size("dp")
    owned_sum = lax.psum_scatter(
        jnp.dot(grad_local, projector, preferred_element_type=jnp.float32),
        ("dp", "mp"),
        scatter_dimension=0,
        tiled=True,
    )
    mean_grad = owned_sum / replicas
    new_moment = 0.9 * moment + 0.1 * mean_grad
    new_second = 0.999 * second + 0.001 * mean_grad * mean_grad
    first_fix = 1.0 - 0.9**ADAM_STEP
    second_fix = 1.0 - 0.999**ADAM_STEP
    direction = (new_moment / first_fix / (jnp.sqrt(new_second / second_fix) + 1e-08)).astype(
        jnp.bfloat16
    )
    update = decode_rows(lax.all_gather(direction, ("dp", "mp"), axis=0, tiled=True), projector)
    return (new_moment, new_second, update)


def solution(mesh):
    return jax.shard_map(
        shards,
        mesh=mesh,
        in_specs=(P("dp", None, "mp"), P("mp", None), P(("dp", "mp"), None), P(("dp", "mp"), None)),
        out_specs=(P(("dp", "mp"), None), P(("dp", "mp"), None), P(None, "mp")),
        check_vma=False,
    )
```

profile of v0, /device:TPU:1, one launch (start us, length us, event | category | flops | bytes accessed | tf_op | source)
XLA Modules:
  0.0 1032.5 jit_solution(7509915883668910526)
XLA Ops:
  7.2 0.0 copy-start
  7.2 0.0 reduce-scatter.2.cloned.1.call-start
  7.2 1.5 copy-done
  8.8 14.5 %fusion = f32[4096,1024]{1,0:T(8,128)} fusion(bf16[1024,1024]{1,0:T(8,128)(2,1)S(1)} %copy-done, bf16[1,4096,1024]{2,1,0:T(8,128)(2,1)} %param.4), kind=kOutput, calls=%fused_computation | convolution fusion | flops 8589934592 | bytes 27262976 | tf_op jit(solution)/shard_map/dot_general | solution.py:19
  23.2 0.0 copy-start.1
  23.2 0.0 copy-start.2
  23.2 0.0 reduce-scatter.2.cloned.1.call-update
  23.3 0.0 all-gather.2.cloned.1.call-start
  23.3 663.7 %reduce-scatter.2.cloned.1.call-done = f32[32,1024]{1,0:T(8,128)} async-done(((f32[4096,1024]{1,0:T(8,128)}), f32[32,1024]{1,0:T(8,128)}) %reduce-scatter.2.cloned.1.call-update) | async-done | bytes 131088 | tf_op jit(solution)/shard_map/reduce_scatter | solution.py:18
  687.0 0.0 copy-done.1
  687.1 0.0 copy-done.2
  687.1 1.7 divide_convert_fusion
  688.7 0.0 all-gather.2.cloned.1.call-update
  688.7 322.3 %all-gather.2.cloned.1.call-done = bf16[4096,1024]{1,0:T(8,128)(2,1)} async-done(((bf16[32,1024]{1,0:T(8,128)(2,1)}), bf16[4096,1024]{1,0:T(8,128)(2,1)}) %all-gather.2.cloned.1.call-update) | async-done | bytes 8388624 | tf_op jit(solution)/shard_map/all_gather | solution.py:32
  1011.1 14.6 %convolution_convert_fusion = bf16[4096,1024]{1,0:T(8,128)(2,1)} fusion(bf16[4096,1024]{1,0:T(8,128)(2,1)} %all-gather.2.cloned.1.call-done, bf16[1024,1024]{1,0:T(8,128)(2,1)S(1)} %copy-done), kind=kOutput, calls=%fused_computation.2 | convolution fusion | flops 8594128896 | bytes 18874368 | tf_op jit(solution)/shard_map/dot_general | solution.py:10
Async XLA Ops:
  7.2 1.6 copy-start
  7.2 679.9 %reduce-scatter.2.cloned.1.call-start = ((), (), s32[]{:S(2)}) async-start(), calls=%async_computation.1 | async-start | bytes 16908288 | tf_op jit(solution)/shard_map/reduce_scatter | solution.py:18
  23.2 663.8 %copy-start.1 = (f32[32,1024]{1,0:T(8,128)S(1)}, f32[32,1024]{1,0:T(8,128)}, u32[]{:S(2)}) copy-start(f32[32,1024]{1,0:T(8,128)} %param.7) | copy-start | bytes 393220
  23.2 663.8 %copy-start.2 = (f32[32,1024]{1,0:T(8,128)S(1)}, f32[32,1024]{1,0:T(8,128)}, u32[]{:S(2)}) copy-start(f32[32,1024]{1,0:T(8,128)} %param.6) | copy-start | bytes 393220
  23.3 987.8 %all-gather.2.cloned.1.call-start = ((), (), s32[]{:S(2)}) async-start(), calls=%async_computation.2 | async-start | bytes 8454144 | tf_op jit(solution)/shard_map/all_gather | solution.py:32
Sparse Core Ops, SparseCore 0:
  23.4 663.6 reduce-scatter.1
  689.3 321.7 all-gather.1
where the time goes:
time: 1030 us
  waiting for transfers between devices  986 us (96%)
  matrix products  29 us (3%)
  between operations  14 us (1%)
    reduce_scatter x1, waiting for transfers between devices, shards(): lax.psum_scatter(jnp.dot(grad_local, projector, preferred_element_type=jn...  664 us
    all_gather x1, waiting for transfers between devices, shards(): lax.all_gather(direction, ('dp', 'mp'), axis=0, tiled=True)  322 us
  transfers between devices with their start and end apart: 2, of which 2 were waited for; matrix products, arithmetic and copies ran while one was open for 0% of the time, Pallas kernels for 0%

commit v1 on v0

v1 whole, which is shorter than its diff:
```python
import functools

import jax
import jax.numpy as jnp
from jax import lax
from jax.experimental import pallas as pl
from jax.experimental.pallas import tpu as pltpu
from jax.sharding import PartitionSpec as P

ADAM_STEP = 10
FIRST_FIX = 1.0 - 0.9**ADAM_STEP
SECOND_FIX = 1.0 - 0.999**ADAM_STEP
MESH = pl.DeviceIdType.MESH
PARTS = ((0, 384, (0, 2, 1)), (384, 384, (1, 2, 0)), (768, 256, (2, 1, 0)))
LO, HI = slice(0, 2), slice(2, 4)
ALL = slice(None)


def position():
    dp, mp = lax.axis_index("dp"), lax.axis_index("mp")
    x = (mp // 4) * 2 + (dp // 2) % 2
    return [x, dp // 4, mp % 4], dp % 2


def device(chip, core):
    x, y, z = chip
    return {"dp": (y * 2 + x % 2) * 2 + core, "mp": (x // 2) * 4 + z}


def adam(total, moment, second):
    mean_grad = total / 16.0
    new_moment = 0.9 * moment + 0.1 * mean_grad
    new_second = 0.999 * second + 0.001 * mean_grad * mean_grad
    direction = new_moment / FIRST_FIX / (jnp.sqrt(new_second / SECOND_FIX) + 1e-08)
    return new_moment, new_second, direction.astype(jnp.bfloat16)


def kernel(
    g_hbm, p_hbm, m_hbm, v_hbm,
    nm_out, nv_out, up_out,
    gs, gr, pv, mv, vv, part, rf, n1, n2, n3, dirs, stage,
    lsem, xs_sem, xr_sem, rs_s, rs_r, ag_s, ag_r, out_l, out_s, out_r,
):
    me, core = position()

    def shifted(axis, by):
        chip = list(me)
        chip[axis] = (me[axis] + by) % 4
        return chip

    def remote(src, dst, ssem, rsem, chip, to_core):
        return pltpu.make_async_remote_copy(
            src, dst, ssem, rsem, device_id=device(chip, to_core), device_id_type=MESH
        )

    def at(axes, first, third, second, block=slice(None)):
        idx = [None, None, None]
        idx[axes[0]], idx[axes[1]], idx[axes[2]] = first, second, third
        return tuple(idx)

    x_order = [(me[0] + k) % 4 for k in (2, 1, 3, 0)]
    y_order = [(me[1] + k) % 4 for k in (2, 1, 3, 0)]
    blocks = [(x_order[0], y) for y in y_order]
    blocks += [(x, y_order[0]) for x in x_order[1:]]
    blocks += [(x, y) for x in x_order[1:] for y in y_order[1:]]

    own_load, exchange = [], []
    load_p = pltpu.make_async_copy(p_hbm, pv, lsem.at[16])
    load_m = pltpu.make_async_copy(m_hbm, mv, lsem.at[17])
    load_v = pltpu.make_async_copy(v_hbm, vv, lsem.at[18])
    for i, (x, y) in enumerate(blocks):
        cp = pltpu.make_async_copy(g_hbm.at[y, x % 2, core, x // 2], gs.at[x, y], lsem.at[i])
        cp.start()
        own_load.append(cp)
        if i == 3:
            load_p.start()
    load_m.start()
    load_v.start()

    barrier = pltpu.get_barrier_semaphore()
    friends = [(shifted(a, k), core) for a in range(3) for k in (1, 2, 3)] + [(me, 1 - core)]
    for chip, to_core in friends:
        pl.semaphore_signal(barrier, inc=1, device_id=device(chip, to_core), device_id_type=MESH)
    pl.semaphore_wait(barrier, len(friends))

    for i, (x, y) in enumerate(blocks):
        cp = remote(
            g_hbm.at[y, x % 2, 1 - core, x // 2], gr.at[x, y], xs_sem.at[i], xr_sem.at[i], me, 1 - core
        )
        cp.start()
        exchange.append(cp)

    def pair_sum(i):
        x, y = blocks[i]
        own_load[i].wait()
        exchange[i].wait_recv()

        @pl.loop(0, 4)
        def _(z):
            gs[x, y, z] = gs[x, y, z] + gr[x, y, z]

    def project(p, k):
        c0, w, axes = PARTS[p]
        idx = [ALL, ALL, ALL]
        idx[axes[0]] = (me[axes[0]] + k) % 4
        rows = gs[tuple(idx)].reshape(512, 1024)
        out = jnp.dot(rows, pv[:, c0 : c0 + w], preferred_element_type=jnp.float32)
        part[tuple(idx) + (ALL, slice(c0, c0 + w))] = out.astype(jnp.bfloat16).reshape(4, 4, 32, w)

    waits = []
    count = [0, 0]

    def rs_send(src, dst, p, axis, by):
        k = count[0]
        count[0] += 1
        cp = remote(src, dst, rs_s.at[k], rs_r.at[k], shifted(axis, by), core)
        cp.start()
        waits.append(cp)
        return cp

    def ag_send(ref_at, axis, by):
        k = count[1]
        count[1] += 1
        cp = remote(dirs.at[ref_at], dirs.at[ref_at], ag_s.at[k], ag_r.at[k], shifted(axis, by), core)
        cp.start()
        waits.append(cp)
        return cp

    def cols(p):
        return pl.ds(PARTS[p][0], PARTS[p][1])

    def vcols(p):
        return slice(PARTS[p][0], PARTS[p][0] + PARTS[p][1])

    def pos(p, k):
        return (me[PARTS[p][2][0]] + k) % 4

    def far(p):
        axes = PARTS[p][2]
        c = cols(p)
        i = at(axes, pos(p, 2), LO, ALL) + (ALL, c)
        j = at(axes, pos(p, 2), HI, ALL) + (ALL, c)
        up = rs_send(part.at[i], rf.at[0, :, :, :, c], p, axes[0], 1)
        down = rs_send(part.at[j], rf.at[1, :, :, :, c], p, axes[0], 3)
        return [up, down]

    def near_plain(p, k):
        axes = PARTS[p][2]
        c = cols(p)
        half = HI if k == 1 else LO
        i = at(axes, pos(p, k), half, ALL) + (ALL, c)
        return rs_send(part.at[i], n1.at[0 if k == 1 else 1, half, :, :, c], p, axes[0], k)

    def near_relay(p, k, arrived):
        axes = PARTS[p][2]
        c, vc = cols(p), vcols(p)
        half = LO if k == 1 else HI
        slot = 0 if k == 1 else 1
        first = pos(p, k)
        arrived.wait_recv()

        @pl.loop(0, 8)
        def _(i):
            t, s = i // 4, i % 4
            a = at(axes, first, t + half.start, s)
            mine = part[a + (ALL, vc)].astype(jnp.float32)
            part[a + (ALL, vc)] = (mine + rf[slot, t, s, :, vc].astype(jnp.float32)).astype(jnp.bfloat16)

        i = at(axes, first, half, ALL) + (ALL, c)
        return rs_send(part.at[i], n1.at[slot, half, :, :, c], p, axes[0], k)

    f32 = lambda v: v.astype(jnp.float32)

    def second_stage(p, arrived):
        axes = PARTS[p][2]
        c, vc = cols(p), vcols(p)
        for cp in arrived:
            cp.wait_recv()

        @pl.loop(0, 16)
        def _(i):
            t, s = i // 4, i % 4
            a = at(axes, me[axes[0]], t, s) + (ALL, vc)
            part[a] = (f32(part[a]) + f32(n1[0, t, s, :, vc]) + f32(n1[1, t, s, :, vc])).astype(jnp.bfloat16)

        out = []
        for k in (2, 1, 3):
            i = at(axes, me[axes[0]], ALL, (me[axes[1]] + k) % 4) + (ALL, c)
            out.append(rs_send(part.at[i], n2.at[k - 1, :, :, c], p, axes[1], k))
        return out

    def third_stage(p, arrived):
        axes = PARTS[p][2]
        c, vc = cols(p), vcols(p)
        for cp in arrived:
            cp.wait_recv()

        @pl.loop(0, 4)
        def _(t):
            a = at(axes, me[axes[0]], t, me[axes[1]]) + (ALL, vc)
            part[a] = (
                f32(part[a]) + f32(n2[0, t, :, vc]) + f32(n2[1, t, :, vc]) + f32(n2[2, t, :, vc])
            ).astype(jnp.bfloat16)

        out = []
        for k in (2, 1, 3):
            i = at(axes, me[axes[0]], (me[axes[2]] + k) % 4, me[axes[1]]) + (ALL, c)
            out.append(rs_send(part.at[i], n3.at[k - 1, :, c], p, axes[2], k))
        return out

    def step_and_gather(p, arrived):
        axes = PARTS[p][2]
        c, vc = cols(p), vcols(p)
        for cp in arrived:
            cp.wait_recv()
        mine = tuple(me)
        total = f32(part[mine + (ALL, vc)]) + f32(n3[0, :, vc]) + f32(n3[1, :, vc]) + f32(n3[2, :, vc])
        new_moment, new_second, direction = adam(total, mv[:, vc], vv[:, vc])
        nm_out[:, vc] = new_moment
        nv_out[:, vc] = new_second
        dirs[mine + (ALL, vc)] = direction
        return [ag_send(mine + (ALL, c), axes[2], k) for k in (2, 1, 3)]

    def gather_second(p, arrived):
        axes = PARTS[p][2]
        for cp in arrived:
            cp.wait_recv()
        i = at(axes, me[axes[0]], ALL, me[axes[1]]) + (ALL, cols(p))
        return [ag_send(i, axes[1], k) for k in (2, 1, 3)]

    def gather_first(p, arrived):
        axes = PARTS[p][2]
        for cp in arrived:
            cp.wait_recv()
        c = cols(p)
        lo = at(axes, me[axes[0]], LO, ALL) + (ALL, c)
        hi = at(axes, me[axes[0]], HI, ALL) + (ALL, c)
        up, down = ag_send(lo, axes[0], 1), ag_send(hi, axes[0], 3)
        rest = [ag_send(hi, axes[0], 1), ag_send(lo, axes[0], 3)]
        return up, down, rest

    def gather_relay(p, up, down):
        axes = PARTS[p][2]
        c = cols(p)
        up.wait_recv()
        a = ag_send(at(axes, pos(p, 3), LO, ALL) + (ALL, c), axes[0], 1)
        down.wait_recv()
        b = ag_send(at(axes, pos(p, 1), HI, ALL) + (ALL, c), axes[0], 3)
        return [a, b]

    for i in range(4):
        pair_sum(i)
    load_p.wait()
    project(0, 2)
    far_a = far(0)
    for i in range(4, 7):
        pair_sum(i)
    project(1, 2)
    far_b = far(1)
    near = [[], [], []]
    for i in range(7, 10):
        pair_sum(i)
    project(0, 1)
    near[0].append(near_plain(0, 1))
    for i in range(10, 13):
        pair_sum(i)
    project(0, 3)
    near[0].append(near_plain(0, 3))
    for i in range(13, 16):
        pair_sum(i)
    project(2, 2)
    far_c = far(2)
    project(1, 1)
    near[1].append(near_plain(1, 1))
    project(1, 3)
    near[1].append(near_plain(1, 3))
    near[0].append(near_relay(0, 1, far_a[0]))
    near[0].append(near_relay(0, 3, far_a[1]))
    project(2, 1)
    near[2].append(near_plain(2, 1))
    project(2, 3)
    near[2].append(near_plain(2, 3))
    near[1].append(near_relay(1, 1, far_b[0]))
    near[1].append(near_relay(1, 3, far_b[1]))
    project(0, 0)
    near[2].append(near_relay(2, 1, far_c[0]))
    near[2].append(near_relay(2, 3, far_c[1]))
    project(1, 0)
    project(2, 0)

    second = [second_stage(p, near[p]) for p in range(3)]
    third = [third_stage(p, second[p]) for p in range(3)]
    load_m.wait()
    load_v.wait()
    g3 = [step_and_gather(p, third[p]) for p in range(3)]
    g2 = [gather_second(p, g3[p]) for p in range(3)]
    g1 = [gather_first(p, g2[p]) for p in range(3)]
    last = [gather_relay(p, g1[p][0], g1[p][1]) for p in range(3)]
    for p in range(3):
        for cp in g1[p][2] + last[p]:
            cp.wait_recv()

    out_waits = []
    for n, x in enumerate(x_order):
        rows = dirs[x].reshape(512, 1024)
        out = lax.dot_general(rows, pv[...], (((1,), (1,)), ((), ())), preferred_element_type=jnp.float32)
        stage[n] = out.astype(jnp.bfloat16).reshape(4, 4, 32, 1024)
        there = up_out.at[:, x % 2, core, x // 2]
        a = remote(stage.at[n], there, out_s.at[n], out_r.at[n], me, 1 - core)
        a.start()
        b = pltpu.make_async_copy(stage.at[n], there, out_l.at[n])
        b.start()
        out_waits += [a, b]
    for cp in out_waits:
        cp.wait()
    for cp in exchange + waits:
        cp.wait_send()


def shards(grads, projector, moment, second):
    g = grads.reshape(4, 2, 2, 2, 4, 32, 1024)
    bf16 = jnp.bfloat16
    anywhere = pl.BlockSpec(memory_space=pl.ANY)
    vmem = pl.BlockSpec(memory_space=pltpu.VMEM)
    dma = pltpu.SemaphoreType.DMA
    new_moment, new_second, update = pl.pallas_call(
        kernel,
        out_shape=(
            jax.ShapeDtypeStruct((32, 1024), jnp.float32),
            jax.ShapeDtypeStruct((32, 1024), jnp.float32),
            jax.ShapeDtypeStruct((4, 2, 2, 2, 4, 32, 1024), bf16),
        ),
        in_specs=[anywhere] * 4,
        out_specs=(vmem, vmem, anywhere),
        scratch_shapes=[
            pltpu.VMEM((4, 4, 4, 32, 1024), bf16),
            pltpu.VMEM((4, 4, 4, 32, 1024), bf16),
            pltpu.VMEM((1024, 1024), bf16),
            pltpu.VMEM((32, 1024), jnp.float32),
            pltpu.VMEM((32, 1024), jnp.float32),
            pltpu.VMEM((4, 4, 4, 32, 1024), bf16),
            pltpu.VMEM((2, 2, 4, 32, 1024), bf16),
            pltpu.VMEM((2, 4, 4, 32, 1024), bf16),
            pltpu.VMEM((3, 4, 32, 1024), bf16),
            pltpu.VMEM((3, 32, 1024), bf16),
            pltpu.VMEM((4, 4, 4, 32, 1024), bf16),
            pltpu.VMEM((4, 4, 4, 32, 1024), bf16),
            dma((19,)), dma((16,)), dma((16,)), dma((36,)), dma((36,)), dma((36,)), dma((36,)),
            dma((4,)), dma((4,)), dma((4,)),
        ],
        compiler_params=pltpu.CompilerParams(
            collective_id=0, has_side_effects=True, vmem_limit_bytes=48 * 2**20
        ),
        cost_estimate=pl.CostEstimate(flops=9 * 10**9, bytes_accessed=2**24, transcendentals=0),
        name="galore_step",
    )(g, projector, moment, second)
    return new_moment, new_second, update.reshape(4096, 1024)


def solution(mesh):
    return jax.shard_map(
        shards,
        mesh=mesh,
        in_specs=(P("dp", None, "mp"), P("mp", None), P(("dp", "mp"), None), P(("dp", "mp"), None)),
        out_specs=(P(("dp", "mp"), None), P(("dp", "mp"), None), P(None, "mp")),
        check_vma=False,
    )
```

time: 1030 us -> 90.1 us (0.09)
  waiting for transfers between devices: 986 us -> 0 us
  Pallas kernels: 0 us -> 76.7 us
  matrix products: 29 us -> 0 us
  between operations: 14 us -> 0.65 us
  local copies, waits for them, and re-layouts: 1.55 us -> 12.5 us
    reduce_scatter x1 -> x0, waiting for transfers between devices: 664 us -> none  [shards(): lax.psum_scatter(jnp.dot(grad_local, projector, preferred_element_type=jn...]
    all_gather x1 -> x0, waiting for transfers between devices: 322 us -> none  [shards(): lax.all_gather(direction, ('dp', 'mp'), axis=0, tiled=True)]
    pallas_call x0 -> x1, Pallas kernels: none -> 76.7 us  [shards(): pl.pallas_call(kernel, out_shape=(jax.ShapeDtypeStruct((32, 1024), jnp.fl...]
    dot_general x2 -> x0, matrix products: 29 us -> none  [the longest x1 14.6 us: decode_rows(): lax.dot_general(dir_rows, projector, (((1,), (1,)), ((), ())), preferred_...]
    unnamed x6 -> x9, local copies, waits for them, and re-layouts: 1.55 us -> 12.5 us
  transfers between devices with their start and end apart: 2 -> 0, of which waited for: 2 -> 0; matrix products, arithmetic and copies ran while one was open for 0% -> 0% of each run, Pallas kernels for 0% -> 0%
where the time goes in v1:
time: 90.1 us; the launch traced here: 89.9 us
  Pallas kernels  76.7 us (85%)
  local copies, waits for them, and re-layouts  12.5 us (14%)
    pallas_call x1, Pallas kernels, shards(): pl.pallas_call(kernel, out_shape=(jax.ShapeDtypeStruct((32, 1024), jnp.fl...  76.7 us
    unnamed x9, local copies, waits for them, and re-layouts  12.5 us

profile of v1, /device:TPU:1, one launch (start us, length us, event | category | flops | bytes accessed | tf_op | source)
XLA Modules:
  0.0 89.9 jit_solution(7750686353790146301)
XLA Ops:
  0.6 0.0 copy-start
  0.6 1.6 %copy-done = bf16[1024,1024]{1,0:T(8,128)(2,1)S(1)} copy-done((bf16[1024,1024]{1,0:T(8,128)(2,1)S(1)}, bf16[1024,1024]{1,0:T(8,128)(2,1)}, u32[]{:S(2)}) %copy-start) | copy-done | bytes 2097176
  2.2 0.0 copy-start.1
  2.2 0.9 %copy-done.1 = f32[32,1024]{1,0:T(8,128)S(1)} copy-done((f32[32,1024]{1,0:T(8,128)S(1)}, f32[32,1024]{1,0:T(8,128)}, u32[]{:S(2)}) %copy-start.1) | copy-done | bytes 131096
  3.1 0.0 copy-start.2
  3.1 0.9 %copy-done.2 = f32[32,1024]{1,0:T(8,128)S(1)} copy-done((f32[32,1024]{1,0:T(8,128)S(1)}, f32[32,1024]{1,0:T(8,128)}, u32[]{:S(2)}) %copy-start.2) | copy-done | bytes 131096
  4.0 76.7 %galore_step.1 = (f32[32,1024]{1,0:T(8,128)S(1)}, f32[32,1024]{1,0:T(8,128)S(1)}, bf16[4,2,2,2,4,32,1024]{6,5,4,3,2,1,0:T(8,128)(2,1)}) custom-call(bf16[4,2,2,2,4,32,1024]{6,5,4,3,2,1,0:T(8,128)(2,1)} %bitcast.3, bf16[1024,1024]{1,0:T(8,128)(2,1)S(1)} %copy-done, f32[32,1024]{1,0:T(8,128)S(1)} %copy-done.1, f32[32,1024]{1,0:T(8,128)S(1)} %copy-done.2), custom_call_target="tpu_custom_call" | custom-call | flops 8999999488 | bytes 16777216 | tf_op jit(solution)/shard_map/galore_step/pallas_call | solution.py:326
  80.8 0.7 copy.10
  81.4 0.7 copy.11
  82.1 7.8 %copy.12 = bf16[4096,1024]{1,0:T(8,128)(2,1)} copy(bf16[4096,1024]{1,0:T(8,128)(2,1)} %bitcast.2) | data formatting | bytes 16777216
Async XLA Ops:
  0.6 1.6 %copy-start = (bf16[1024,1024]{1,0:T(8,128)(2,1)S(1)}, bf16[1024,1024]{1,0:T(8,128)(2,1)}, u32[]{:S(2)}) copy-start(bf16[1024,1024]{1,0:T(8,128)(2,1)} %p_hbm.1) | copy-start | bytes 6291460
  2.2 0.9 %copy-start.1 = (f32[32,1024]{1,0:T(8,128)S(1)}, f32[32,1024]{1,0:T(8,128)}, u32[]{:S(2)}) copy-start(f32[32,1024]{1,0:T(8,128)} %m_hbm.1) | copy-start | bytes 393220
  3.1 0.9 %copy-start.2 = (f32[32,1024]{1,0:T(8,128)S(1)}, f32[32,1024]{1,0:T(8,128)}, u32[]{:S(2)}) copy-start(f32[32,1024]{1,0:T(8,128)} %v_hbm.1) | copy-start | bytes 393220

commit v2 on v0

v2 whole, which is shorter than its diff:
```python
import jax
import jax.numpy as jnp
from jax import lax
from jax.experimental import pallas as pl
from jax.experimental.pallas import tpu as pltpu
from jax.sharding import PartitionSpec as P

ADAM_STEP = 10
FIRST_FIX = 1.0 - 0.9**ADAM_STEP
SECOND_FIX = 1.0 - 0.999**ADAM_STEP
MESH = pl.DeviceIdType.MESH
PARTS = ((0, 384, (0, 1, 2)), (384, 384, (1, 2, 0)), (768, 256, (2, 0, 1)))
ALL = slice(None)
LO, HI = slice(0, 2), slice(2, 4)


def position():
    dp, mp = lax.axis_index("dp"), lax.axis_index("mp")
    x = (mp // 4) * 2 + (dp // 2) % 2
    return [x, dp // 4, mp % 4], dp % 2


def device(chip, core):
    x, y, z = chip
    return {"dp": (y * 2 + x % 2) * 2 + core, "mp": (x // 2) * 4 + z}


def adam(total, moment, second):
    mean_grad = total / 16.0
    new_moment = 0.9 * moment + 0.1 * mean_grad
    new_second = 0.999 * second + 0.001 * mean_grad * mean_grad
    direction = new_moment / FIRST_FIX / (jnp.sqrt(new_second / SECOND_FIX) + 1e-08)
    return new_moment, new_second, direction.astype(jnp.bfloat16)


def f32(v):
    return v.astype(jnp.float32)


def bf16(v):
    return v.astype(jnp.bfloat16)


def kernel(
    g_hbm, p_hbm, m_hbm, v_hbm,
    nm_out, nv_out, up_out,
    gs, gr, pv, mv, vv, part, rf, n1, n2, n3, dirs,
    lsem, xs_sem, xr_sem, rs_s, rs_r, ag_s, ag_r, out_s, out_r,
):
    me, core = position()
    sent, arrived = [], set()
    count = {"rs": 0, "ag": 0, "out": 0}
    sems = {"rs": (rs_s, rs_r), "ag": (ag_s, ag_r), "out": (out_s, out_r)}

    def chip_at(axis, by):
        chip = list(me)
        chip[axis] = (me[axis] + by) % 4
        return chip

    def send(src, dst, kind, axis, by):
        k = count[kind]
        count[kind] += 1
        chip, to_core = (me, 1 - core) if axis is None else (chip_at(axis, by), core)
        cp = pltpu.make_async_remote_copy(
            src, dst, sems[kind][0].at[k], sems[kind][1].at[k],
            device_id=device(chip, to_core), device_id_type=MESH,
        )
        cp.start()
        sent.append(cp)
        return cp

    def arrive(*copies):
        for cp in copies:
            if id(cp) not in arrived:
                arrived.add(id(cp))
                cp.wait_recv()

    def finish():
        for cp in sent:
            arrive(cp)
            cp.wait_send()
        for cp in local:
            loaded(cp)

    def loaded(cp):
        if id(cp) not in arrived:
            arrived.add(id(cp))
            cp.wait()

    blocks = [(2, 2), (2, 1), (2, 3), (2, 0), (1, 2), (3, 2), (0, 2)]
    blocks += [(x, y) for x in (1, 3, 0) for y in (1, 3, 0)]
    place = [((me[0] + x) % 4, (me[1] + y) % 4) for x, y in blocks]

    local, own = [], []

    def load(src, dst):
        cp = pltpu.make_async_copy(src, dst, lsem.at[len(local)])
        cp.start()
        local.append(cp)
        return cp

    for i, (x, y) in enumerate(blocks):
        own.append(load(g_hbm.at[place[i][1], place[i][0] % 2, core, place[i][0] // 2], gs.at[x, y]))
        if i == 3:
            load_p = load(p_hbm, pv)
    load_m, load_v = load(m_hbm, mv), load(v_hbm, vv)

    barrier = pltpu.get_barrier_semaphore()
    friends = [(chip_at(a, k), core) for a in range(3) for k in (1, 2, 3)] + [(me, 1 - core)]
    for chip, to_core in friends:
        pl.semaphore_signal(barrier, inc=1, device_id=device(chip, to_core), device_id_type=MESH)
    pl.semaphore_wait(barrier, len(friends))

    exchange = []
    for i, (x, y) in enumerate(blocks):
        cp = pltpu.make_async_remote_copy(
            g_hbm.at[place[i][1], place[i][0] % 2, 1 - core, place[i][0] // 2], gr.at[x, y],
            xs_sem.at[i], xr_sem.at[i], device_id=device(me, 1 - core), device_id_type=MESH,
        )
        cp.start()
        sent.append(cp)
        exchange.append(cp)

    def project(first, last):
        rows = []
        for i in range(first, last):
            loaded(own[i])
            arrive(exchange[i])
        for i in range(first, last):
            x, y = blocks[i]
            rows.append((gs[x, y] + gr[x, y]).reshape(128, 1024))
        out = jnp.dot(jnp.concatenate(rows, 0), pv[...], preferred_element_type=jnp.float32)
        for i in range(first, last):
            x, y = blocks[i]
            mine = bf16(out[(i - first) * 128 : (i - first + 1) * 128]).reshape(4, 32, 1024)
            for z in range(4):
                part[x, y, (z - me[2] + 4) % 4] = mine[z]

    def at(p, a1, a2, a3):
        idx = [None, None, None]
        for axis, i in zip(PARTS[p][2], (a1, a2, a3)):
            idx[axis] = i
        return tuple(idx)

    def rest(p, a2, a3):
        _, second, third = PARTS[p][2]
        return (a2, a3) if second < third else (a3, a2)

    def cols(p):
        return (ALL, slice(PARTS[p][0], PARTS[p][0] + PARTS[p][1]))

    far = [{}, {}, {}]
    near = [{LO.start: [], HI.start: []} for _ in PARTS]

    def send_far(p, g):
        axis = PARTS[p][2][0]
        up = send(part.at[at(p, 2, g, LO) + cols(p)], rf.at[(0,) + rest(p, g, LO) + cols(p)], "rs", axis, 1)
        down = send(part.at[at(p, 2, g, HI) + cols(p)], rf.at[(1,) + rest(p, g, HI) + cols(p)], "rs", axis, 3)
        far[p][g.start] = (up, down)

    def send_near(p, by, g, half):
        slot = 0 if by == 1 else 1
        cp = send(
            part.at[at(p, by, g, half) + cols(p)], n1.at[(slot,) + rest(p, g, half) + cols(p)],
            "rs", PARTS[p][2][0], by,
        )
        near[p][g.start].append(cp)

    def send_plain(p, by, g):
        send_near(p, by, g, HI if by == 1 else LO)

    def send_relay(p, g):
        for slot, by, half in ((0, 1, LO), (1, 3, HI)):
            arrive(far[p][g.start][slot])
            i = at(p, by, g, half) + cols(p)
            part[i] = bf16(f32(part[i]) + f32(rf[(slot,) + rest(p, g, half) + cols(p)]))
            send_near(p, by, g, half)

    second = [[], [], []]

    def send_second(p, g):
        arrive(*near[p][g.start])
        i = at(p, 0, g, ALL) + cols(p)
        j = rest(p, g, ALL) + cols(p)
        part[i] = bf16(f32(part[i]) + f32(n1[(0,) + j]) + f32(n1[(1,) + j]))
        for k in range(g.start, g.stop):
            if k:
                src = part.at[at(p, 0, k, ALL) + cols(p)]
                second[p].append(send(src, n2.at[(k - 1, ALL) + cols(p)], "rs", PARTS[p][2][1], k))

    third = [[], [], []]

    def send_third(p):
        arrive(*second[p])
        i = at(p, 0, 0, ALL) + cols(p)
        total = f32(part[i])
        for k in range(3):
            total = total + f32(n2[(k, ALL) + cols(p)])
        part[i] = bf16(total)
        for k in (2, 1, 3):
            src = part.at[at(p, 0, 0, k) + cols(p)]
            third[p].append(send(src, n3.at[(k - 1,) + cols(p)], "rs", PARTS[p][2][2], k))

    def gather(p, kind_axis, src_idx, dst_idx, by):
        return send(dirs.at[src_idx + cols(p)], dirs.at[dst_idx + cols(p)], "ag", kind_axis, by)

    g3, g2 = [[], [], []], [[], [], []]
    pieces = [{}, {}, {}]
    ends = [[], [], []]

    def step(p):
        arrive(*third[p])
        c = cols(p)
        total = f32(part[(0, 0, 0) + c])
        for k in range(3):
            total = total + f32(n3[(k,) + c])
        new_moment, new_second, direction = adam(total, mv[c], vv[c])
        nm_out[c] = new_moment
        nv_out[c] = new_second
        dirs[(0, 0, 0) + c] = direction
        for k in (2, 1, 3):
            g3[p].append(gather(p, PARTS[p][2][2], (0, 0, 0), at(p, 0, 0, 4 - k), k))

    def gather_piece(p, g):
        axis = PARTS[p][2][0]
        up = gather(p, axis, at(p, 0, g, ALL), at(p, 3, g, ALL), 1)
        down = gather(p, axis, at(p, 0, g, ALL), at(p, 1, g, ALL), 3)
        pieces[p][g.start] = (up, down)

    def gather_second(p):
        arrive(*g3[p])
        for k in (2, 1, 3):
            g2[p].append(gather(p, PARTS[p][2][1], at(p, 0, 0, ALL), at(p, 0, 4 - k, ALL), k))
        gather_piece(p, slice(0, 1))

    def gather_first(p):
        arrive(*g2[p])
        gather_piece(p, slice(1, 2))
        gather_piece(p, slice(2, 4))

    def gather_relay(p, g):
        axis = PARTS[p][2][0]
        up, down = pieces[p][g.start]
        arrive(up)
        ends[p].append(gather(p, axis, at(p, 3, g, LO), at(p, 2, g, LO), 1))
        arrive(down)
        ends[p].append(gather(p, axis, at(p, 1, g, HI), at(p, 2, g, HI), 3))

    def decode(rows):
        lhs = jnp.concatenate([dirs[x, y].reshape(128, 1024) for x, y in rows], 0)
        out = lax.dot_general(lhs, pv[...], (((1,), (1,)), ((), ())), preferred_element_type=jnp.float32)
        for i, (x, y) in enumerate(rows):
            mine = bf16(out[i * 128 : (i + 1) * 128]).reshape(4, 32, 1024)
            ax, ay = (me[0] + x) % 4, (me[1] + y) % 4
            for z in range(4):
                up_out[ay, ax % 2, core, ax // 2, (me[2] + z) % 4] = mine[z]
            there = up_out.at[ay, ax % 2, core, ax // 2]
            send(there, there, "out", None, 0)

    loaded(load_p)
    project(0, 4)
    send_far(0, HI)
    send_far(0, LO)
    project(4, 7)
    send_far(1, HI)
    send_far(1, LO)
    project(7, 10)
    send_plain(0, 1, HI)
    project(10, 13)
    send_plain(0, 3, HI)
    project(13, 16)
    send_far(2, HI)
    send_plain(1, 1, HI)
    send_plain(1, 3, HI)
    send_far(2, LO)
    send_relay(0, HI)
    send_plain(2, 1, HI)
    send_plain(2, 3, HI)
    send_plain(0, 1, LO)
    send_plain(0, 3, LO)
    send_relay(1, HI)
    send_plain(1, 1, LO)
    send_plain(1, 3, LO)
    send_relay(0, LO)
    send_relay(2, HI)
    send_plain(2, 1, LO)
    send_plain(2, 3, LO)
    send_relay(1, LO)
    send_relay(2, LO)
    for p in range(3):
        send_second(p, HI)
    for p in range(3):
        send_second(p, LO)
    for p in range(3):
        send_third(p)
    loaded(load_m)
    loaded(load_v)
    for p in range(3):
        step(p)
    for p in range(3):
        gather_second(p)
    for p in range(3):
        gather_first(p)
    for g in (slice(0, 1), slice(1, 2), slice(2, 4)):
        for p in range(3):
            gather_relay(p, g)
    arrive(*ends[2])
    for x in (0, 1, 3):
        decode([(x, y) for y in (0, 1, 3)])
    arrive(*ends[1])
    decode([(x, 2) for x in (0, 1, 3)])
    arrive(*ends[0])
    decode([(2, 0), (2, 1)])
    decode([(2, 2), (2, 3)])
    finish()


def write_out(nm, nv, up, nm_out, nv_out, up_out, sem):
    copies = [
        pltpu.make_async_copy(src, dst, sem.at[i])
        for i, (src, dst) in enumerate(((up, up_out), (nm, nm_out), (nv, nv_out)))
    ]
    for cp in copies:
        cp.start()
    for cp in copies:
        cp.wait()


def shards(grads, projector, moment, second):
    half = jnp.bfloat16
    full = jnp.float32
    operands = [grads.reshape(4, 2, 2, 2, 4, 32, 1024), projector, moment, second]
    operands = [pltpu.with_memory_space_constraint(v, pltpu.HBM) for v in operands]
    anywhere = pl.BlockSpec(memory_space=pl.ANY)
    vmem = pl.BlockSpec(memory_space=pltpu.VMEM)
    dma = pltpu.SemaphoreType.DMA
    results = pl.pallas_call(
        kernel,
        out_shape=(
            pltpu.VMEM((32, 1024), full),
            pltpu.VMEM((32, 1024), full),
            pltpu.VMEM((4, 2, 2, 2, 4, 32, 1024), half),
        ),
        in_specs=[pl.BlockSpec(memory_space=pltpu.HBM)] * 4,
        out_specs=(vmem, vmem, vmem),
        scratch_shapes=[
            pltpu.VMEM((4, 4, 4, 32, 1024), half),
            pltpu.VMEM((4, 4, 4, 32, 1024), half),
            pltpu.VMEM((1024, 1024), half),
            pltpu.VMEM((32, 1024), full),
            pltpu.VMEM((32, 1024), full),
            pltpu.VMEM((4, 4, 4, 32, 1024), half),
            pltpu.VMEM((2, 4, 4, 32, 1024), half),
            pltpu.VMEM((2, 4, 4, 32, 1024), half),
            pltpu.VMEM((3, 4, 32, 1024), half),
            pltpu.VMEM((3, 32, 1024), half),
            pltpu.VMEM((4, 4, 4, 32, 1024), half),
            dma((19,)), dma((16,)), dma((16,)), dma((54,)), dma((54,)), dma((54,)), dma((54,)),
            dma((16,)), dma((16,)),
        ],
        compiler_params=pltpu.CompilerParams(
            collective_id=0, has_side_effects=True, vmem_limit_bytes=44 * 2**20
        ),
        cost_estimate=pl.CostEstimate(flops=9 * 10**9, bytes_accessed=2**24, transcendentals=0),
        name="galore_step",
    )(*operands)
    new_moment, new_second, update = results
    return pl.pallas_call(
        write_out,
        out_shape=(
            jax.ShapeDtypeStruct((32, 1024), full),
            jax.ShapeDtypeStruct((32, 1024), full),
            jax.ShapeDtypeStruct((4096, 1024), half),
        ),
        in_specs=[anywhere] * 3,
        out_specs=(anywhere,) * 3,
        scratch_shapes=[dma((3,))],
        compiler_params=pltpu.CompilerParams(vmem_limit_bytes=2**20),
        name="write_out",
    )(new_moment, new_second, update.reshape(4096, 1024))


def solution(mesh):
    return jax.shard_map(
        shards,
        mesh=mesh,
        in_specs=(P("dp", None, "mp"), P("mp", None), P(("dp", "mp"), None), P(("dp", "mp"), None)),
        out_specs=(P(("dp", "mp"), None), P(("dp", "mp"), None), P(None, "mp")),
        check_vma=False,
    )
```

time: 1030 us -> 74.4 us (0.07)
  waiting for transfers between devices: 986 us -> 0 us
  Pallas kernels: 0 us -> 73.6 us
  matrix products: 29 us -> 0 us
  between operations: 14 us -> 0.64 us
    reduce_scatter x1 -> x0, waiting for transfers between devices: 664 us -> none  [shards(): lax.psum_scatter(jnp.dot(grad_local, projector, preferred_element_type=jn...]
    all_gather x1 -> x0, waiting for transfers between devices: 322 us -> none  [shards(): lax.all_gather(direction, ('dp', 'mp'), axis=0, tiled=True)]
    pallas_call x0 -> x2, Pallas kernels: none -> 73.6 us  [the longest x1 70.2 us: shards(): pl.pallas_call(kernel, out_shape=(pltpu.VMEM((32, 1024), full), pltpu.VME...]
    dot_general x2 -> x0, matrix products: 29 us -> none  [the longest x1 14.6 us: decode_rows(): lax.dot_general(dir_rows, projector, (((1,), (1,)), ((), ())), preferred_...]
  transfers between devices with their start and end apart: 2 -> 0, of which waited for: 2 -> 0; matrix products, arithmetic and copies ran while one was open for 0% -> 0% of each run, Pallas kernels for 0% -> 0%
where the time goes in v2:
time: 74.4 us; the launch traced here: 74.3 us
  Pallas kernels  73.6 us (99%)
    pallas_call x1, Pallas kernels, shards(): pl.pallas_call(kernel, out_shape=(pltpu.VMEM((32, 1024), full), pltpu.VME...  70.2 us
    pallas_call x1, Pallas kernels, shards(): pl.pallas_call(write_out, out_shape=(jax.ShapeDtypeStruct((32, 1024), ful...  3.48 us

profile of v2, /device:TPU:1, one launch (start us, length us, event | category | flops | bytes accessed | tf_op | source)
XLA Modules:
  0.0 74.3 jit_solution(2157174356818230894)
XLA Ops:
  0.6 70.2 %galore_step.1 = (f32[32,1024]{1,0:T(8,128)S(1)}, f32[32,1024]{1,0:T(8,128)S(1)}, bf16[4,2,2,2,4,32,1024]{6,5,4,3,2,1,0:T(8,128)(2,1)S(1)}) custom-call(bf16[4,2,2,2,4,32,1024]{6,5,4,3,2,1,0:T(8,128)(2,1)} %bitcast.3, bf16[1024,1024]{1,0:T(8,128)(2,1)} %p_hbm.1, f32[32,1024]{1,0:T(8,128)} %m_hbm.1, f32[32,1024]{1,0:T(8,128)} %v_hbm.1), custom_call_target="tpu_custom_call" | custom-call | flops 8999999488 | bytes 16777216 | tf_op jit(solution)/shard_map/galore_step/pallas_call | solution.py:337
  70.8 3.5 %write_out.1 = (f32[32,1024]{1,0:T(8,128)}, f32[32,1024]{1,0:T(8,128)}, bf16[4096,1024]{1,0:T(8,128)(2,1)}) custom-call(f32[32,1024]{1,0:T(8,128)S(1)} %get-tuple-element.6.nm, f32[32,1024]{1,0:T(8,128)S(1)} %get-tuple-element.7.nv, bf16[4096,1024]{1,0:T(8,128)(2,1)S(1)} %bitcast.2), custom_call_target="tpu_custom_call" | custom-call | tf_op jit(solution)/shard_map/write_out/pallas_call | solution.py:368

commit v3 on v2

--- a/solution.py
+++ b/solution.py
@@ -16,13 +16,13 @@
 
 def position():
     dp, mp = lax.axis_index("dp"), lax.axis_index("mp")
-    x = (mp // 4) * 2 + (dp // 2) % 2
-    return [x, dp // 4, mp % 4], dp % 2
+    x = lax.div(mp, 4) * 2 + lax.rem(lax.div(dp, 2), 2)
+    return [x, lax.div(dp, 4), lax.rem(mp, 4)], lax.rem(dp, 2)
 
 
 def device(chip, core):
     x, y, z = chip
-    return {"dp": (y * 2 + x % 2) * 2 + core, "mp": (x // 2) * 4 + z}
+    return {"dp": (y * 2 + lax.rem(x, 2)) * 2 + core, "mp": lax.div(x, 2) * 4 + z}
 
 
 def adam(total, moment, second):
@@ -52,18 +52,23 @@
     count = {"rs": 0, "ag": 0, "out": 0}
     sems = {"rs": (rs_s, rs_r), "ag": (ag_s, ag_r), "out": (out_s, out_r)}
 
-    def chip_at(axis, by):
-        chip = list(me)
-        chip[axis] = (me[axis] + by) % 4
-        return chip
+    ahead = [[lax.rem(m + k, 4) for k in range(4)] for m in me]
+    x_lo, x_hi = [lax.rem(x, 2) for x in ahead[0]], [lax.div(x, 2) for x in ahead[0]]
+    z_place = [lax.rem(z + 4 - me[2], 4) for z in range(4)]
+    peers = {None: device(me, 1 - core)}
+    for axis in range(3):
+        for by in (1, 2, 3):
+            chip = list(me)
+            chip[axis] = ahead[axis][by]
+            peers[axis, by] = device(chip, core)
 
     def send(src, dst, kind, axis, by):
         k = count[kind]
         count[kind] += 1
-        chip, to_core = (me, 1 - core) if axis is None else (chip_at(axis, by), core)
+        peer = peers[None if axis is None else (axis, by)]
         cp = pltpu.make_async_remote_copy(
             src, dst, sems[kind][0].at[k], sems[kind][1].at[k],
-            device_id=device(chip, to_core), device_id_type=MESH,
+            device_id=peer, device_id_type=MESH,
         )
         cp.start()
         sent.append(cp)
@@ -89,8 +94,10 @@
 
     blocks = [(2, 2), (2, 1), (2, 3), (2, 0), (1, 2), (3, 2), (0, 2)]
     blocks += [(x, y) for x in (1, 3, 0) for y in (1, 3, 0)]
-    place = [((me[0] + x) % 4, (me[1] + y) % 4) for x, y in blocks]
-
+
+    barrier = pltpu.get_barrier_semaphore()
+    for peer in peers.values():
+        pl.semaphore_signal(barrier, inc=1, device_id=peer, device_id_type=MESH)
     local, own = [], []
 
     def load(src, dst):
@@ -100,22 +107,18 @@
         return cp
 
     for i, (x, y) in enumerate(blocks):
-        own.append(load(g_hbm.at[place[i][1], place[i][0] % 2, core, place[i][0] // 2], gs.at[x, y]))
+        own.append(load(g_hbm.at[ahead[1][y], x_lo[x], core, x_hi[x]], gs.at[x, y]))
         if i == 3:
             load_p = load(p_hbm, pv)
     load_m, load_v = load(m_hbm, mv), load(v_hbm, vv)
 
-    barrier = pltpu.get_barrier_semaphore()
-    friends = [(chip_at(a, k), core) for a in range(3) for k in (1, 2, 3)] + [(me, 1 - core)]
-    for chip, to_core in friends:
-        pl.semaphore_signal(barrier, inc=1, device_id=device(chip, to_core), device_id_type=MESH)
-    pl.semaphore_wait(barrier, len(friends))
+    pl.semaphore_wait(barrier, len(peers))
 
     exchange = []
     for i, (x, y) in enumerate(blocks):
         cp = pltpu.make_async_remote_copy(
-            g_hbm.at[place[i][1], place[i][0] % 2, 1 - core, place[i][0] // 2], gr.at[x, y],
-            xs_sem.at[i], xr_sem.at[i], device_id=device(me, 1 - core), device_id_type=MESH,
+            g_hbm.at[ahead[1][y], x_lo[x], 1 - core, x_hi[x]], gr.at[x, y],
+            xs_sem.at[i], xr_sem.at[i], device_id=peers[None], device_id_type=MESH,
         )
         cp.start()
         sent.append(cp)
@@ -134,7 +137,7 @@
             x, y = blocks[i]
             mine = bf16(out[(i - first) * 128 : (i - first + 1) * 128]).reshape(4, 32, 1024)
             for z in range(4):
-                part[x, y, (z - me[2] + 4) % 4] = mine[z]
+                part[x, y, z_place[z]] = mine[z]
 
     def at(p, a1, a2, a3):
         idx = [None, None, None]
@@ -235,8 +238,7 @@
 
     def gather_first(p):
         arrive(*g2[p])
-        gather_piece(p, slice(1, 2))
-        gather_piece(p, slice(2, 4))
+        gather_piece(p, slice(1, 4))
 
     def gather_relay(p, g):
         axis = PARTS[p][2][0]
@@ -251,10 +253,9 @@
         out = lax.dot_general(lhs, pv[...], (((1,), (1,)), ((), ())), preferred_element_type=jnp.float32)
         for i, (x, y) in enumerate(rows):
             mine = bf16(out[i * 128 : (i + 1) * 128]).reshape(4, 32, 1024)
-            ax, ay = (me[0] + x) % 4, (me[1] + y) % 4
             for z in range(4):
-                up_out[ay, ax % 2, core, ax // 2, (me[2] + z) % 4] = mine[z]
-            there = up_out.at[ay, ax % 2, core, ax // 2]
+                up_out[ahead[1][y], x_lo[x], core, x_hi[x], ahead[2][z]] = mine[z]
+            there = up_out.at[ahead[1][y], x_lo[x], core, x_hi[x]]
             send(there, there, "out", None, 0)
 
     loaded(load_p)
@@ -301,8 +302,8 @@
         gather_second(p)
     for p in range(3):
         gather_first(p)
-    for g in (slice(0, 1), slice(1, 2), slice(2, 4)):
-        for p in range(3):
+    for g in (slice(0, 1), slice(1, 4)):
+        for p in (2, 0, 1):
             gather_relay(p, g)
     arrive(*ends[2])
     for x in (0, 1, 3):

time: 74.4 us -> 69.9 us (0.940)
  Pallas kernels: 73.6 us -> 69.2 us
    pallas_call x1, Pallas kernels: 70.2 us -> 65.7 us  [shards(): pl.pallas_call(kernel, out_shape=(pltpu.VMEM((32, 1024), full), pltpu.VME...]
where the time goes in v3:
time: 69.9 us; the launch traced here: 69.8 us
  Pallas kernels  69.2 us (99%)
    pallas_call x1, Pallas kernels, shards(): pl.pallas_call(kernel, out_shape=(pltpu.VMEM((32, 1024), full), pltpu.VME...  65.7 us
    pallas_call x1, Pallas kernels, shards(): pl.pallas_call(write_out, out_shape=(jax.ShapeDtypeStruct((32, 1024), ful...  3.48 us

profile of v3, /device:TPU:1, one launch (start us, length us, event | category | flops | bytes accessed | tf_op | source)
XLA Modules:
  0.0 69.8 jit_solution(2439485940036777510)
XLA Ops:
  0.6 65.7 %galore_step.1 = (f32[32,1024]{1,0:T(8,128)S(1)}, f32[32,1024]{1,0:T(8,128)S(1)}, bf16[4,2,2,2,4,32,1024]{6,5,4,3,2,1,0:T(8,128)(2,1)S(1)}) custom-call(bf16[4,2,2,2,4,32,1024]{6,5,4,3,2,1,0:T(8,128)(2,1)} %bitcast.3, bf16[1024,1024]{1,0:T(8,128)(2,1)} %p_hbm.1, f32[32,1024]{1,0:T(8,128)} %m_hbm.1, f32[32,1024]{1,0:T(8,128)} %v_hbm.1), custom_call_target="tpu_custom_call" | custom-call | flops 8999999488 | bytes 16777216 | tf_op jit(solution)/shard_map/galore_step/pallas_call | solution.py:338
  66.3 3.5 %write_out.1 = (f32[32,1024]{1,0:T(8,128)}, f32[32,1024]{1,0:T(8,128)}, bf16[4096,1024]{1,0:T(8,128)(2,1)}) custom-call(f32[32,1024]{1,0:T(8,128)S(1)} %get-tuple-element.6.nm, f32[32,1024]{1,0:T(8,128)S(1)} %get-tuple-element.7.nv, bf16[4096,1024]{1,0:T(8,128)(2,1)S(1)} %bitcast.2), custom_call_target="tpu_custom_call" | custom-call | tf_op jit(solution)/shard_map/write_out/pallas_call | solution.py:369

commit v4 on v3

--- a/solution.py
+++ b/solution.py
@@ -92,7 +92,7 @@
             arrived.add(id(cp))
             cp.wait()
 
-    blocks = [(2, 2), (2, 1), (2, 3), (2, 0), (1, 2), (3, 2), (0, 2)]
+    blocks = [(2, 2), (2, 3), (1, 2), (3, 2), (0, 2), (2, 1), (2, 0)]
     blocks += [(x, y) for x in (1, 3, 0) for y in (1, 3, 0)]
 
     barrier = pltpu.get_barrier_semaphore()
@@ -108,7 +108,7 @@
 
     for i, (x, y) in enumerate(blocks):
         own.append(load(g_hbm.at[ahead[1][y], x_lo[x], core, x_hi[x]], gs.at[x, y]))
-        if i == 3:
+        if i == 1:
             load_p = load(p_hbm, pv)
     load_m, load_v = load(m_hbm, mv), load(v_hbm, vv)
 
@@ -259,12 +259,13 @@
             send(there, there, "out", None, 0)
 
     loaded(load_p)
-    project(0, 4)
+    project(0, 2)
     send_far(0, HI)
-    send_far(0, LO)
-    project(4, 7)
+    project(2, 5)
     send_far(1, HI)
     send_far(1, LO)
+    project(5, 7)
+    send_far(0, LO)
     project(7, 10)
     send_plain(0, 1, HI)
     project(10, 13)
@@ -277,21 +278,23 @@
     send_relay(0, HI)
     send_plain(2, 1, HI)
     send_plain(2, 3, HI)
+    send_relay(1, HI)
     send_plain(0, 1, LO)
     send_plain(0, 3, LO)
-    send_relay(1, HI)
     send_plain(1, 1, LO)
     send_plain(1, 3, LO)
+    send_relay(2, HI)
     send_relay(0, LO)
-    send_relay(2, HI)
     send_plain(2, 1, LO)
     send_plain(2, 3, LO)
     send_relay(1, LO)
     send_relay(2, LO)
-    for p in range(3):
-        send_second(p, HI)
-    for p in range(3):
-        send_second(p, LO)
+    send_second(0, HI)
+    send_second(1, HI)
+    send_second(2, HI)
+    send_second(0, LO)
+    send_second(1, LO)
+    send_second(2, LO)
     for p in range(3):
         send_third(p)
     loaded(load_m)
@@ -308,11 +311,11 @@
     arrive(*ends[2])
     for x in (0, 1, 3):
         decode([(x, y) for y in (0, 1, 3)])
+    arrive(*ends[0])
+    decode([(2, y) for y in (0, 1, 3)])
     arrive(*ends[1])
-    decode([(x, 2) for x in (0, 1, 3)])
-    arrive(*ends[0])
-    decode([(2, 0), (2, 1)])
-    decode([(2, 2), (2, 3)])
+    decode([(0, 2), (1, 2)])
+    decode([(3, 2), (2, 2)])
     finish()
 
 

time: 69.9 us -> 68.8 us (0.984)
  Pallas kernels: 69.2 us -> 68.1 us
    pallas_call x1, Pallas kernels: 65.7 us -> 64.6 us  [shards(): pl.pallas_call(kernel, out_shape=(pltpu.VMEM((32, 1024), full), pltpu.VME...]
where the time goes in v4:
time: 68.8 us; the launch traced here: 68.7 us
  Pallas kernels  68.1 us (99%)
    pallas_call x1, Pallas kernels, shards(): pl.pallas_call(kernel, out_shape=(pltpu.VMEM((32, 1024), full), pltpu.VME...  64.6 us
    pallas_call x1, Pallas kernels, shards(): pl.pallas_call(write_out, out_shape=(jax.ShapeDtypeStruct((32, 1024), ful...  3.48 us

profile of v4, /device:TPU:1, one launch (start us, length us, event | category | flops | bytes accessed | tf_op | source)
XLA Modules:
  0.0 68.7 jit_solution(16795379598446543679)
XLA Ops:
  0.6 64.6 %galore_step.1 = (f32[32,1024]{1,0:T(8,128)S(1)}, f32[32,1024]{1,0:T(8,128)S(1)}, bf16[4,2,2,2,4,32,1024]{6,5,4,3,2,1,0:T(8,128)(2,1)S(1)}) custom-call(bf16[4,2,2,2,4,32,1024]{6,5,4,3,2,1,0:T(8,128)(2,1)} %bitcast.3, bf16[1024,1024]{1,0:T(8,128)(2,1)} %p_hbm.1, f32[32,1024]{1,0:T(8,128)} %m_hbm.1, f32[32,1024]{1,0:T(8,128)} %v_hbm.1), custom_call_target="tpu_custom_call" | custom-call | flops 8999999488 | bytes 16777216 | tf_op jit(solution)/shard_map/galore_step/pallas_call | solution.py:341
  65.2 3.5 %write_out.1 = (f32[32,1024]{1,0:T(8,128)}, f32[32,1024]{1,0:T(8,128)}, bf16[4096,1024]{1,0:T(8,128)(2,1)}) custom-call(f32[32,1024]{1,0:T(8,128)S(1)} %get-tuple-element.6.nm, f32[32,1024]{1,0:T(8,128)S(1)} %get-tuple-element.7.nv, bf16[4096,1024]{1,0:T(8,128)(2,1)S(1)} %bitcast.2), custom_call_target="tpu_custom_call" | custom-call | tf_op jit(solution)/shard_map/write_out/pallas_call | solution.py:372

commit v5 on v4

--- a/solution.py
+++ b/solution.py
@@ -226,9 +226,20 @@
 
     def gather_piece(p, g):
         axis = PARTS[p][2][0]
-        up = gather(p, axis, at(p, 0, g, ALL), at(p, 3, g, ALL), 1)
-        down = gather(p, axis, at(p, 0, g, ALL), at(p, 1, g, ALL), 3)
+        if g.start == 0:
+            up = gather(p, axis, at(p, 0, g, ALL), at(p, 3, g, ALL), 1)
+            down = gather(p, axis, at(p, 0, g, ALL), at(p, 1, g, ALL), 3)
+        else:
+            up = gather(p, axis, at(p, 0, g, LO), at(p, 3, g, LO), 1)
+            down = gather(p, axis, at(p, 0, g, HI), at(p, 1, g, HI), 3)
         pieces[p][g.start] = (up, down)
+
+    others = []
+
+    def gather_others(p, g):
+        axis = PARTS[p][2][0]
+        others.append(gather(p, axis, at(p, 0, g, HI), at(p, 3, g, HI), 1))
+        others.append(gather(p, axis, at(p, 0, g, LO), at(p, 1, g, LO), 3))
 
     def gather_second(p):
         arrive(*g3[p])
@@ -305,9 +316,13 @@
         gather_second(p)
     for p in range(3):
         gather_first(p)
-    for g in (slice(0, 1), slice(1, 4)):
-        for p in (2, 0, 1):
-            gather_relay(p, g)
+    for p in (2, 0, 1):
+        gather_relay(p, slice(0, 1))
+    for p in (2, 0, 1):
+        gather_others(p, slice(1, 4))
+    for p in (2, 0, 1):
+        gather_relay(p, slice(1, 4))
+    arrive(*others)
     arrive(*ends[2])
     for x in (0, 1, 3):
         decode([(x, y) for y in (0, 1, 3)])

time: 68.8 us -> 69.5 us (1.010)
  Pallas kernels: 68.1 us -> 68.8 us
    pallas_call x1, Pallas kernels: 64.6 us -> 65.3 us  [shards(): pl.pallas_call(kernel, out_shape=(pltpu.VMEM((32, 1024), full), pltpu.VME...]
where the time goes in v5:
time: 69.5 us; the launch traced here: 69.4 us
  Pallas kernels  68.8 us (99%)
    pallas_call x1, Pallas kernels, shards(): pl.pallas_call(kernel, out_shape=(pltpu.VMEM((32, 1024), full), pltpu.VME...  65.3 us
    pallas_call x1, Pallas kernels, shards(): pl.pallas_call(write_out, out_shape=(jax.ShapeDtypeStruct((32, 1024), ful...  3.48 us

profile of v5, /device:TPU:1, one launch (start us, length us, event | category | flops | bytes accessed | tf_op | source)
XLA Modules:
  0.0 69.4 jit_solution(1073915939260699579)
XLA Ops:
  0.6 65.3 %galore_step.1 = (f32[32,1024]{1,0:T(8,128)S(1)}, f32[32,1024]{1,0:T(8,128)S(1)}, bf16[4,2,2,2,4,32,1024]{6,5,4,3,2,1,0:T(8,128)(2,1)S(1)}) custom-call(bf16[4,2,2,2,4,32,1024]{6,5,4,3,2,1,0:T(8,128)(2,1)} %bitcast.3, bf16[1024,1024]{1,0:T(8,128)(2,1)} %p_hbm.1, f32[32,1024]{1,0:T(8,128)} %m_hbm.1, f32[32,1024]{1,0:T(8,128)} %v_hbm.1), custom_call_target="tpu_custom_call" | custom-call | flops 8999999488 | bytes 16777216 | tf_op jit(solution)/shard_map/galore_step/pallas_call | solution.py:356
  65.9 3.5 %write_out.1 = (f32[32,1024]{1,0:T(8,128)}, f32[32,1024]{1,0:T(8,128)}, bf16[4096,1024]{1,0:T(8,128)(2,1)}) custom-call(f32[32,1024]{1,0:T(8,128)S(1)} %get-tuple-element.6.nm, f32[32,1024]{1,0:T(8,128)S(1)} %get-tuple-element.7.nv, bf16[4096,1024]{1,0:T(8,128)(2,1)S(1)} %bitcast.2), custom_call_target="tpu_custom_call" | custom-call | tf_op jit(solution)/shard_map/write_out/pallas_call | solution.py:387
